TPU v7x, 32 devices: a whole 2x2x4 slice. The times are simulated.
32 devices in a mesh: group: 2 (over y), blk: 4 (over z), own: 4 (over x, core).
Axes of the slice: x: 2, y: 2, z: 4, core: 2. Of those that a mesh axis runs over, the one named last changes fastest.
Arguments:
- activations: bfloat16 [1, 1024, 28672], P(None, ('group', 'blk'), 'own'), parts along dimension 1, may hold values from -6 to 6
- rank_grads: bfloat16 [1, 1024, 16], P(None, ('group', 'blk')), parts along dimension 1, may hold values from -1.1953125 to 1.1953125
- lengths: int32 [1, 8, 2], P(None, ('group', 'blk')), parts along dimension 1, may hold values from 1 to 96, 128 in all within a row
- adapter_ids: int32 [1, 16], P(None, 'group'), parts along dimension 1, may hold values from 0 to 3, as said below
- input_basis: bfloat16 [128, 28672], P(('group', 'blk'), 'own'), parts along dimension 0, may hold values from -0.03125 to 0.03125
- rank_basis: float32 [8, 16, 16], P('group'), parts along dimension 0, may hold values from -1.5 to 1.5
- prior_values: float32 [8, 16, 64], P('group', None, ('blk', 'own')), parts along dimension 0, may hold values from 0.5 to 4
Outputs:
- eigenvalues: float32 [8, 16, 64], P('group', None, ('blk', 'own')), parts along dimension 0
There are 2 independent parts, one for each index of `group`. A program takes and returns all parts, laid end to end along the dimension named above; each array names one. Nothing has to cross between parts.
Inputs may be any that keep to these rules, and one draw needn't show every extreme that they name: `adapter_ids`: every one of the 4 adapters names at least one sequence of every step.
All inputs are finite; a program needn't handle non-finite values.
Results may differ from a plain program's by a relative error of at most 0.0003.
Values may be sent and summed in bfloat16 or wider, within the bound.
A program may use at most 128 MiB of HBM per device.

v0:
```python
import jax
import jax.numpy as jnp
from jax import lax
from jax.sharding import PartitionSpec as P

forget_rate = 0.5


def rank_weights(rank_grads, lengths, local_ids, rank_basis):
    token_count = rank_grads.shape[1]
    adapter_count = rank_basis.shape[0]
    seq_ends = jnp.cumsum(lengths, axis=1)
    starts = seq_ends - lengths
    positions = jnp.arange(token_count, dtype=jnp.int32)
    member = ((positions >= starts[..., None]) & (positions < seq_ends[..., None])).astype(
        jnp.float32
    )
    onehot = (local_ids[..., None] == jnp.arange(adapter_count, dtype=jnp.int32)).astype(
        jnp.float32
    )
    seq_basis = jnp.einsum("sna,aqr->snqr", onehot, rank_basis, precision=lax.Precision.HIGHEST)
    projected = jnp.einsum(
        "stq,snqr->snrt", rank_grads.astype(jnp.float32), seq_basis, precision=lax.Precision.HIGHEST
    )
    return projected * member[:, :, None, :]


def per_device(
    activations, rank_grads, lengths, adapter_ids, input_basis, rank_basis, prior_values
):
    step_count, token_count, inner_count = activations.shape
    seq_count = lengths.shape[2]
    adapter_count = rank_basis.shape[0]
    rank_count = rank_basis.shape[1]
    col_count = input_basis.shape[0]
    own_count = lax.axis_size("own")
    blk_count = lax.axis_size("blk")
    share_cols = col_count // own_count
    row_total = step_count * seq_count * rank_count
    blk_index = lax.axis_index("blk")
    local_ids = lax.dynamic_slice_in_dim(adapter_ids, blk_index * seq_count, seq_count, 1)
    weights = rank_weights(rank_grads, lengths[:, 0, :], local_ids, rank_basis)

    def make_rotate(source_rows):
        flat_rows = source_rows.reshape(step_count * token_count, source_rows.shape[2])

        def rotate(panel_piece):
            rotated = lax.dot_general(
                flat_rows, panel_piece, (((1,), (1,)), ((), ())), preferred_element_type=jnp.float32
            )
            rotated = rotated.reshape(step_count, token_count, panel_piece.shape[0])
            seq_sums = jnp.einsum(
                "snrt,stc->snrc", weights, rotated, precision=lax.Precision.HIGHEST
            )
            return seq_sums.reshape(row_total, panel_piece.shape[0])

        return rotate

    rotate_part = make_rotate(activations)
    panel_piece = lax.all_gather(input_basis, "blk", axis=0, tiled=True)
    groups = panel_piece.shape[0] // col_count
    seq_sums = rotate_part(panel_piece).reshape(row_total, groups, own_count, share_cols)
    placed = jnp.transpose(seq_sums, (2, 0, 1, 3)).reshape(
        own_count, row_total, groups * share_cols
    )
    rank_rows = lax.psum_scatter(placed, "own", scatter_dimension=0, tiled=True)[0]
    squares = (rank_rows * rank_rows).reshape(
        step_count, seq_count, rank_count, blk_count * share_cols
    )
    adapter_range = jnp.arange(adapter_count, dtype=jnp.int32)
    counts = jnp.sum((adapter_ids[..., None] == adapter_range).astype(jnp.float32), axis=1)
    local_onehot = (local_ids[..., None] == adapter_range).astype(jnp.float32)
    step_scale = (1.0 - forget_rate) * forget_rate ** jnp.arange(
        step_count - 1, -1, -1, dtype=jnp.float32
    )
    share_weights = local_onehot * (step_scale[:, None, None] / counts[:, None, :])
    adapter_part = jnp.einsum(
        "sna,snrc->arc", share_weights, squares, precision=lax.Precision.HIGHEST
    )
    summed = lax.psum_scatter(adapter_part, "blk", scatter_dimension=2, tiled=True)
    return summed + forget_rate**step_count * prior_values


def solution(mesh):
    return jax.shard_map(
        per_device,
        mesh=mesh,
        in_specs=(
            P(None, ("group", "blk"), "own"),
            P(None, ("group", "blk"), None),
            P(None, ("group", "blk"), None),
            P(None, "group"),
            P(("group", "blk"), "own"),
            P("group", None, None),
            P("group", None, ("blk", "own")),
        ),
        out_specs=P("group", None, ("blk", "own")),
        check_vma=False,
    )
```

profile of v0, /device:TPU:0, one launch (start us, length us, event | category | flops | bytes accessed | tf_op | source)
XLA Modules:
  0.0 82.5 jit_solution(3512065109585274106)
XLA Ops:
  6.5 0.0 copy-start
  6.5 0.0 reduce-scatter.2.cloned.1.call-start
  6.6 1.0 %reduce-window.6 = s32[2,1]{0,1:T(1,128)S(1)} reduce-window(s32[2,1]{0,1:T(1,128)} %bitcast.43, s32[]{:T(128)} %constant.8.clone.1), window={size=2x1 pad=1_0x0_0}, to_apply=%region_1.2 | reduce-window | flops 2 | bytes 20 | tf_op jit(solution)/shard_map/reduce-window.1
  7.5 0.7 bitcast_subtract_fusion
  8.2 23.0 %all_gather.3 = bf16[64,7168]{1,0:T(8,128)(2,1)S(1)} all-gather(bf16[16,7168]{1,0:T(8,128)(2,1)} %param.11), channel_id=1, replica_groups=mesh['group'=2,'blk'=4,'own'=4] {'blk'}, dimensions={0}, use_global_device_ids=true | all-gather | bytes 1146880 | tf_op jit(solution)/shard_map/all_gather | solution.py:60
  31.1 1.3 %dot_general.22 = bf16[4,4,4,7168]{3,2,1,0:T(4,128)(2,1)} reshape(bf16[64,7168]{1,0:T(8,128)(2,1)S(1)} %all_gather.3) | data formatting | bytes 1835008 | tf_op jit(solution)/shard_map/dot_general | solution.py:48
  32.4 0.0 copy-done.4
  32.4 0.1 dynamic-slice_bitcast_fusion
  32.5 0.2 fusion.2
  32.7 0.1 and_convert_fusion
  32.8 2.0 %fusion = f32[4,4,4,128]{3,2,1,0:T(4,128)S(1)} fusion(bf16[4,4,4,7168]{3,2,1,0:T(4,128)(2,1)} %dot_general.22, bf16[1,128,7168]{2,1,0:T(8,128)(2,1)S(1)} %copy-done), kind=kOutput, calls=%fused_computation | convolution fusion | flops 117440512 | bytes 2785280 | tf_op jit(solution)/shard_map/dot_general | solution.py:48
  34.8 0.0 copy-done.2
  34.8 0.2 convolution_multiply_fusion
  35.0 0.2 convolution_bitcast_fusion
  35.2 0.6 copy.25
  35.8 0.0 reduce-scatter.2.cloned.1.call-update
  35.8 0.1 convert_reduce_fusion
  36.0 0.6 dynamic-slice
  37.2 17.7 %reduce-scatter.2.cloned.1.call-done = f32[1,32,16]{1,2,0:T(8,128)} async-done(((f32[4,32,16]{1,2,0:T(8,128)}), f32[1,32,16]{1,2,0:T(8,128)}) %reduce-scatter.2.cloned.1.call-update) | async-done | bytes 2064 | tf_op jit(solution)/shard_map/reduce_scatter | solution.py:66
  54.9 0.8 mul.40
  55.7 0.1 mul.41
  55.7 0.3 fusion.7
  56.1 19.0 %all-reduce = f32[4,16,16]{1,0,2:T(4,128)S(1)} all-reduce(f32[4,16,16]{1,0,2:T(4,128)S(1)} %fusion.7), channel_id=3, replica_groups=mesh['group'=2,'blk'=4,'own'=4] {'blk'}, use_global_device_ids=true, to_apply=%region_3.4.clone | all-reduce | flops 1024 | bytes 8192
  75.1 0.6 copy.29
  (11 shorter events, 0.0 us)
Async XLA Ops:
  6.5 26.2 %copy-start = (bf16[1,128,7168]{2,1,0:T(8,128)(2,1)S(1)}, bf16[1,128,7168]{2,1,0:T(8,128)(2,1)}, u32[]{:S(2)}) copy-start(bf16[1,128,7168]{2,1,0:T(8,128)(2,1)} %param.7) | copy-start | bytes 5505028
  6.5 25.8 %copy-start.4 = (s32[1,8]{1,0:T(1,128)S(1)}, s32[1,8]{1,0:T(1,128)}, u32[]{:S(2)}) copy-start(s32[1,8]{1,0:T(1,128)} %param.10) | copy-start | bytes 100
  6.5 25.9 %copy-start.3 = (f32[4,16,16]{2,1,0:T(8,128)S(1)}, f32[4,16,16]{2,1,0:T(8,128)}, u32[]{:S(2)}) copy-start(f32[4,16,16]{2,1,0:T(8,128)} %param.12) | copy-start | bytes 12292
  6.5 48.4 %reduce-scatter.2.cloned.1.call-start = ((), (), s32[]{:S(2)}) async-start(), calls=%async_computation.1 | async-start | bytes 40960 | tf_op jit(solution)/shard_map/reduce_scatter | solution.py:66
  32.4 2.4 %copy-start.2 = (bf16[1,128,16]{1,2,0:T(8,128)(2,1)S(1)}, bf16[1,128,16]{1,2,0:T(8,128)(2,1)}, u32[]{:S(2)}) copy-start(bf16[1,128,16]{1,2,0:T(8,128)(2,1)} %param.8) | copy-start | bytes 12292
  32.8 3.2 %copy-start.5 = (u32[32]{0:T(128)S(1)}, u32[32]{0:T(128)}, u32[]{:S(2)}) copy-start(u32[32]{0:T(128)} %constant.28) | copy-start | bytes 388
  32.8 42.3 %copy-start.1 = (f32[4,16,4]{1,2,0:T(4,128)S(1)}, f32[4,16,4]{1,2,0:T(4,128)}, u32[]{:S(2)}) copy-start(f32[4,16,4]{1,2,0:T(4,128)} %param.13) | copy-start | bytes 3076
Sparse Core Ops, SparseCore 0:
  36.0 18.8 reduce-scatter.1
where the time goes:
time: 82.9 us; the launch traced here: 82.5 us
  blocking collectives  41.9 us (51%)
  waiting for transfers between devices  17.7 us (21%)
  between operations  14.1 us (17%)
  local copies, waits for them, and re-layouts  3.23 us (4%)
  matrix products  2.95 us (4%)
  other arithmetic  2.6 us (3%)
    all_gather x1, blocking collectives, per_device(): panel_piece = lax.all_gather(input_basis, 'blk', axis=0, tiled=True)  23 us
    unnamed x1, blocking collectives  19 us
    reduce_scatter x1, waiting for transfers between devices, per_device(): lax.psum_scatter(placed, 'own', scatter_dimension=0, tiled=True)[0]  17.7 us
    dot_general x1, matrix products, rotate(): lax.dot_general(flat_rows, panel_piece, (((1,), (1,)), ((), ())), preferr...  2.01 us
  transfers between devices with their start and end apart: 1, of which 1 were waited for; matrix products, arithmetic and copies ran while one was open for 1% of the time, Pallas kernels for 0%

commit v1 on v0

v1 whole, which is shorter than its diff:
```python
import functools

import jax
import jax.numpy as jnp
from jax import lax
from jax.experimental import pallas as pl
from jax.experimental.pallas import tpu as pltpu
from jax.sharding import PartitionSpec as P

forget_rate = 0.5
HIGHEST = lax.Precision.HIGHEST
MESH = pl.DeviceIdType.MESH


def kernel(
    n, own_n, chunks,
    lengths, ids, acts_hbm, grads, basis_hbm, rank_basis, out,
    acts, panel, rot, part, part_in, sq, sq_in, load_sem, rs, rr, ls, lr, s1, r1, s2, r2,
):
    z = lax.axis_index("blk")
    o = lax.axis_index("own")
    tokens, width = acts.shape
    cols = panel.shape[1]
    share = cols // own_n
    wide = width // chunks
    seqs = lengths.shape[2]
    adapters, rank = rank_basis.shape[0], rank_basis.shape[1]
    lanes = seqs * adapters * rank
    half = adapters * rank

    load_acts = pltpu.make_async_copy(acts_hbm.at[0], acts, load_sem.at[0])
    load_acts.start()
    load_own = pltpu.make_async_copy(basis_hbm, panel.at[z], load_sem.at[1])
    load_own.start()

    barrier = pltpu.get_barrier_semaphore()

    def greet_blk(k, carry):
        pl.semaphore_signal(
            barrier, inc=1, device_id={"blk": lax.rem(z + k, n)}, device_id_type=MESH
        )
        return carry

    lax.fori_loop(1, n, greet_blk, 0)
    for k in range(1, own_n):
        pl.semaphore_signal(
            barrier, inc=1, device_id={"own": lax.rem(o + k, own_n)}, device_id_type=MESH
        )
    pl.semaphore_wait(barrier, n - 1 + own_n - 1)

    def piece(c):
        return pl.ds(c * wide, wide)

    def right(s, c, first=False):
        at = (slice(None), piece(c))
        block = z - s
        return pltpu.make_async_remote_copy(
            src_ref=basis_hbm.at[at] if first else panel.at[(block,) + at],
            dst_ref=panel.at[(block,) + at],
            send_sem=rs.at[s, c], recv_sem=rr.at[s, c],
            device_id={"blk": z + 1}, device_id_type=MESH,
        )

    def left(s, c, first=False):
        at = (slice(None), piece(c))
        block = z + s
        return pltpu.make_async_remote_copy(
            src_ref=basis_hbm.at[at] if first else panel.at[(block,) + at],
            dst_ref=panel.at[(block,) + at],
            send_sem=ls.at[s, c], recv_sem=lr.at[s, c],
            device_id={"blk": z - 1}, device_id_type=MESH,
        )

    def from_left(s, c):
        dst = panel.at[z - 1 - s, :, piece(c)]
        return pltpu.make_async_remote_copy(
            src_ref=dst, dst_ref=dst, send_sem=rs.at[s, c], recv_sem=rr.at[s, c],
            device_id={"blk": z - 1}, device_id_type=MESH,
        )

    def from_right(s, c):
        dst = panel.at[z + 1 + s, :, piece(c)]
        return pltpu.make_async_remote_copy(
            src_ref=dst, dst_ref=dst, send_sem=ls.at[s, c], recv_sem=lr.at[s, c],
            device_id={"blk": z + 1}, device_id_type=MESH,
        )

    for c in range(chunks):
        @pl.when(z < n - 1)
        def _():
            right(0, c, True).start()

        @pl.when(z > 0)
        def _():
            left(0, c, True).start()

    lane = lax.broadcasted_iota(jnp.int32, (1, lanes), 1)
    lane_seq = lane // half
    lane_adapter = lax.rem(lane // rank, adapters)
    lane_id = jnp.zeros((1, lanes), jnp.int32)
    lane_start = jnp.zeros((1, lanes), jnp.int32)
    lane_end = jnp.zeros((1, lanes), jnp.int32)
    start = jnp.int32(0)
    for q in range(seqs):
        end = start + lengths[0, 0, q]
        here = lane_seq == q
        lane_id = jnp.where(here, ids[0, z * seqs + q], lane_id)
        lane_start = jnp.where(here, start, lane_start)
        lane_end = jnp.where(here, end, lane_end)
        start = end

    def count(k, total):
        return total + jnp.where(lane_adapter == ids[0, k], 1.0, 0.0)

    counts = lax.fori_loop(0, ids.shape[1], count, jnp.zeros((1, lanes), jnp.float32))
    scale = (1.0 - forget_rate) / counts
    spread = jnp.concatenate([rank_basis[a] for a in range(adapters)] * seqs, axis=1)
    spread = jnp.where(lane_id == lane_adapter, spread, 0.0)
    weights = jnp.dot(
        grads[0].astype(jnp.float32), spread, precision=HIGHEST,
        preferred_element_type=jnp.float32,
    )
    token = lax.broadcasted_iota(jnp.int32, (tokens, lanes), 0)
    weights = jnp.where((token >= lane_start) & (token < lane_end), weights, 0.0)

    def rotate(block, c):
        return lax.dot_general(
            acts[:, c * wide:(c + 1) * wide], panel[block, :, c * wide:(c + 1) * wide],
            (((1,), (1,)), ((), ())), preferred_element_type=jnp.float32,
        )

    def add(block, c):
        value = rotate(block, c)
        if c > 0:
            value = value + rot[block]
        if c < chunks - 1:
            rot[block] = value
        else:
            sums = lax.dot_general(
                value, weights, (((0,), (0,)), ((), ())), precision=HIGHEST,
                preferred_element_type=jnp.float32,
            )
            for k in range(own_n):
                part[k, block] = sums[k * share:(k + 1) * share]

    load_acts.wait()
    load_own.wait()
    for c in range(chunks):
        add(z, c)

    def step(s):
        for c in range(chunks):
            @pl.when(z - 1 - s >= 0)
            def _():
                from_left(s, c).wait_recv()

                @pl.when(z < n - 1)
                def _():
                    right(s + 1, c).start()

            @pl.when(z + 1 + s < n)
            def _():
                from_right(s, c).wait_recv()

                @pl.when(z > 0)
                def _():
                    left(s + 1, c).start()

            @pl.when(z - 1 - s >= 0)
            def _():
                add(z - 1 - s, c)

            @pl.when(z + 1 + s < n)
            def _():
                add(z + 1 + s, c)

    def settle(s):
        for c in range(chunks):
            @pl.when((z - s >= 0) & (z < n - 1))
            def _():
                right(s, c).wait_send()

            @pl.when((z + s < n) & (z > 0))
            def _():
                left(s, c).wait_send()

    def over_steps(f):
        if n <= 8:
            for s in range(n - 1):
                f(s)
        else:
            lax.fori_loop(0, n - 1, lambda s, carry: (f(s), carry)[1], 0)

    over_steps(step)

    def give(k):
        to = lax.rem(o + k, own_n)
        return pltpu.make_async_remote_copy(
            src_ref=part.at[to], dst_ref=part_in.at[k - 1], send_sem=s1.at[k - 1],
            recv_sem=r1.at[k - 1], device_id={"own": to}, device_id_type=MESH,
        )

    for k in range(1, own_n):
        give(k).start()
    total = part[o]
    for k in range(1, own_n):
        give(k).wait_recv()
        total = total + part_in[k - 1]
    squares = total * total * scale
    folded = squares
    for q in range(1, seqs):
        folded = folded + pltpu.roll(squares, q * half, 2)
    sq[...] = folded

    def give_sq(k):
        to = lax.rem(z + k, n)
        return pltpu.make_async_remote_copy(
            src_ref=sq.at[to], dst_ref=sq_in.at[k - 1], send_sem=s2.at[k - 1],
            recv_sem=r2.at[k - 1], device_id={"blk": to}, device_id_type=MESH,
        )

    if n <= 8:
        for k in range(1, n):
            give_sq(k).start()
        result = sq[z]
        for k in range(1, n):
            give_sq(k).wait_recv()
            result = result + sq_in[k - 1]
        for k in range(1, n):
            give_sq(k).wait_send()
    else:
        def begin(k, carry):
            give_sq(k).start()
            return carry

        def gather(k, value):
            give_sq(k).wait_recv()
            return value + sq_in[k - 1]

        def end(k, carry):
            give_sq(k).wait_send()
            return carry

        lax.fori_loop(1, n, begin, 0)
        result = lax.fori_loop(1, n, gather, sq[z])
        lax.fori_loop(1, n, end, 0)
    out[...] = result
    for k in range(1, own_n):
        give(k).wait_send()
    over_steps(settle)


def per_device(
    activations, rank_grads, lengths, adapter_ids, input_basis, rank_basis, prior_values
):
    n, own_n = lax.axis_size("blk"), lax.axis_size("own")
    tokens, width = activations.shape[1:]
    cols = input_basis.shape[0]
    share = cols // own_n
    seqs = lengths.shape[2]
    adapters, rank = rank_basis.shape[:2]
    lanes = seqs * adapters * rank
    chunks = 4 if n <= 8 else 1
    vmem = pl.BlockSpec(memory_space=pltpu.VMEM)
    smem = pl.BlockSpec(memory_space=pltpu.SMEM)
    anywhere = pl.BlockSpec(memory_space=pl.ANY)
    dma = pltpu.SemaphoreType.DMA
    f32 = jnp.float32
    sums = pl.pallas_call(
        functools.partial(kernel, n, own_n, chunks),
        out_shape=jax.ShapeDtypeStruct((share, lanes), f32),
        in_specs=[smem, smem, anywhere, vmem, anywhere, vmem],
        out_specs=vmem,
        scratch_shapes=[
            pltpu.VMEM((tokens, width), jnp.bfloat16),
            pltpu.VMEM((n, cols, width), jnp.bfloat16),
            pltpu.VMEM((n, tokens, cols), f32),
            pltpu.VMEM((own_n, n, share, lanes), f32),
            pltpu.VMEM((own_n - 1, n, share, lanes), f32),
            pltpu.VMEM((n, share, lanes), f32),
            pltpu.VMEM((n - 1, share, lanes), f32),
            dma((2,)),
            dma((n - 1, chunks)), dma((n - 1, chunks)),
            dma((n - 1, chunks)), dma((n - 1, chunks)),
            dma((own_n - 1,)), dma((own_n - 1,)),
            dma((n - 1,)), dma((n - 1,)),
        ],
        compiler_params=pltpu.CompilerParams(
            collective_id=0, has_side_effects=True, vmem_limit_bytes=48 << 20
        ),
    )(lengths, adapter_ids, activations, rank_grads, input_basis, rank_basis)
    mean_sq = sums[:, :adapters * rank].T.reshape(adapters, rank, share)
    return mean_sq + forget_rate * prior_values


def solution(mesh):
    return jax.shard_map(
        per_device,
        mesh=mesh,
        in_specs=(
            P(None, ("group", "blk"), "own"),
            P(None, ("group", "blk"), None),
            P(None, ("group", "blk"), None),
            P(None, "group"),
            P(("group", "blk"), "own"),
            P("group", None, None),
            P("group", None, ("blk", "own")),
        ),
        out_specs=P("group", None, ("blk", "own")),
        check_vma=False,
    )
```

time: 82.9 us -> 35.5 us (0.43)
  blocking collectives: 41.9 us -> 0 us
  Pallas kernels: 0 us -> 29.1 us
  waiting for transfers between devices: 17.7 us -> 0 us
  between operations: 14.1 us -> 0.03 us
  matrix products: 2.95 us -> 0 us
  local copies, waits for them, and re-layouts: 3.23 us -> 5.41 us
  other arithmetic: 2.6 us -> 0.61 us
    pallas_call x0 -> x1, Pallas kernels: none -> 29.1 us  [per_device(): pl.pallas_call(functools.partial(kernel, n, own_n, chunks), out_shape=jax...]
    all_gather x1 -> x0, blocking collectives: 23 us -> none  [per_device(): panel_piece = lax.all_gather(input_basis, 'blk', axis=0, tiled=True)]
    unnamed x1 -> x0, blocking collectives: 19 us -> none
    reduce_scatter x1 -> x0, waiting for transfers between devices: 17.7 us -> none  [per_device(): lax.psum_scatter(placed, 'own', scatter_dimension=0, tiled=True)[0]]
    unnamed x13, local copies, waits for them, and re-layouts: 0.61 us -> 5.32 us
    dot_general x5 -> x0, matrix products: 2.95 us -> none  [the longest x1 2.01 us: rotate(): lax.dot_general(flat_rows, panel_piece, (((1,), (1,)), ((), ())), preferr...]
    dot_general x1 -> x0, local copies, waits for them, and re-layouts: 1.26 us -> none  [rotate(): lax.dot_general(flat_rows, panel_piece, (((1,), (1,)), ((), ())), preferr...]
    another operation x1 -> x0, other arithmetic: 0.96 us -> none
  transfers between devices with their start and end apart: 1 -> 0, of which waited for: 1 -> 0; matrix products, arithmetic and copies ran while one was open for 1% -> 0% of each run, Pallas kernels for 0% -> 0%
where the time goes in v1:
time: 35.5 us; the launch traced here: 35.2 us
  Pallas kernels  29.1 us (82%)
  local copies, waits for them, and re-layouts  5.41 us (15%)
  other arithmetic  0.61 us (2%)
    pallas_call x1, Pallas kernels, per_device(): pl.pallas_call(functools.partial(kernel, n, own_n, chunks), out_shape=jax...  29.1 us
    unnamed x13, local copies, waits for them, and re-layouts  5.32 us

profile of v1, /device:TPU:0, one launch (start us, length us, event | category | flops | bytes accessed | tf_op | source)
XLA Modules:
  0.0 35.2 jit_solution(16599852985908064296)
XLA Ops:
  0.0 0.0 copy-start.5
  0.0 0.8 %copy.8.grads = bf16[1,128,16]{2,1,0:T(8,128)(2,1)S(1)} copy(bf16[1,128,16]{1,2,0:T(8,128)(2,1)} %param.8) | data formatting | bytes 8192 | tf_op args[1]
  0.8 0.0 copy-start
  0.8 1.5 %copy-done = bf16[1,128,7168]{2,1,0:T(8,128)(2,1)S(1)} copy-done((bf16[1,128,7168]{2,1,0:T(8,128)(2,1)S(1)}, bf16[1,128,7168]{2,1,0:T(8,128)(2,1)}, u32[]{:S(2)}) %copy-start) | copy-done | bytes 1835032
  2.3 0.0 copy-start.1
  2.3 0.9 %copy-done.1 = bf16[16,7168]{1,0:T(8,128)(2,1)S(1)} copy-done((bf16[16,7168]{1,0:T(8,128)(2,1)S(1)}, bf16[16,7168]{1,0:T(8,128)(2,1)}, u32[]{:S(2)}) %copy-start.1) | copy-done | bytes 229400
  3.3 0.0 copy-start.2
  3.3 0.8 %copy-done.2 = f32[4,16,16]{2,1,0:T(8,128)S(1)} copy-done((f32[4,16,16]{2,1,0:T(8,128)S(1)}, f32[4,16,16]{2,1,0:T(8,128)}, u32[]{:S(2)}) %copy-start.2) | copy-done | bytes 4120
  4.0 0.0 copy-start.3
  4.0 0.7 %copy-done.3 = s32[1,1,2]{2,1,0:T(1,128)S(1)} copy-done((s32[1,1,2]{2,1,0:T(1,128)S(1)}, s32[1,1,2]{2,1,0:T(1,128)}, u32[]{:S(2)}) %copy-start.3) | copy-done | bytes 32
  4.7 0.0 copy-start.4
  4.7 0.7 %copy-done.4 = s32[1,8]{1,0:T(1,128)S(1)} copy-done((s32[1,8]{1,0:T(1,128)S(1)}, s32[1,8]{1,0:T(1,128)}, u32[]{:S(2)}) %copy-start.4) | copy-done | bytes 56
  5.3 29.1 %shard_map.73 = f32[4,128]{1,0:T(4,128)S(1)} custom-call(s32[1,1,2]{2,1,0:T(1,128)S(1)} %copy-done.3, s32[1,8]{1,0:T(1,128)S(1)} %copy-done.4, bf16[1,128,7168]{2,1,0:T(8,128)(2,1)S(1)} %copy-done, bf16[1,128,16]{2,1,0:T(8,128)(2,1)S(1)} %copy.8.grads, bf16[16,7168]{1,0:T(8,128)(2,1)S(1)} %copy-done.1, f32[4,16,16]{2,1,0:T(8,128)S(1)} %copy-done.2), custom_call_target="tpu_custom_call" | custom-call | tf_op jit(solution)/shard_map/pallas_call | solution.py:269
  34.5 0.1 reshape.3
  34.6 0.0 copy-done.5
  34.6 0.6 %copy_add_fusion = f32[4,16,4]{1,2,0:T(4,128)} fusion(f32[4,16,4]{1,0,2:T(4,128)S(1)} %reshape.3, f32[4,16,4]{1,2,0:T(4,128)S(1)} %copy-done.5), kind=kLoop, calls=%fused_computation | loop fusion | flops 512 | bytes 3072 | tf_op jit(solution)/shard_map/add | solution.py:293
  (1 shorter events, 0.0 us)
Async XLA Ops:
  0.0 34.6 %copy-start.5 = (f32[4,16,4]{1,2,0:T(4,128)S(1)}, f32[4,16,4]{1,2,0:T(4,128)}, u32[]{:S(2)}) copy-start(f32[4,16,4]{1,2,0:T(4,128)} %param.13) | copy-start | bytes 3076
  0.8 1.5 %copy-start = (bf16[1,128,7168]{2,1,0:T(8,128)(2,1)S(1)}, bf16[1,128,7168]{2,1,0:T(8,128)(2,1)}, u32[]{:S(2)}) copy-start(bf16[1,128,7168]{2,1,0:T(8,128)(2,1)} %acts_hbm.1) | copy-start | bytes 5505028
  2.3 0.9 %copy-start.1 = (bf16[16,7168]{1,0:T(8,128)(2,1)S(1)}, bf16[16,7168]{1,0:T(8,128)(2,1)}, u32[]{:S(2)}) copy-start(bf16[16,7168]{1,0:T(8,128)(2,1)} %basis_hbm.1) | copy-start | bytes 688132
  3.3 0.8 %copy-start.2 = (f32[4,16,16]{2,1,0:T(8,128)S(1)}, f32[4,16,16]{2,1,0:T(8,128)}, u32[]{:S(2)}) copy-start(f32[4,16,16]{2,1,0:T(8,128)} %rank_basis.1) | copy-start | bytes 12292
  4.0 0.7 %copy-start.3 = (s32[1,1,2]{2,1,0:T(1,128)S(1)}, s32[1,1,2]{2,1,0:T(1,128)}, u32[]{:S(2)}) copy-start(s32[1,1,2]{2,1,0:T(1,128)} %lengths.1) | copy-start | bytes 28
  4.7 0.7 %copy-start.4 = (s32[1,8]{1,0:T(1,128)S(1)}, s32[1,8]{1,0:T(1,128)}, u32[]{:S(2)}) copy-start(s32[1,8]{1,0:T(1,128)} %ids.1) | copy-start | bytes 100

commit v2 on v1

--- a/solution.py
+++ b/solution.py
@@ -14,8 +14,8 @@
 
 def kernel(
     n, own_n, chunks,
-    lengths, ids, acts_hbm, grads, basis_hbm, rank_basis, out,
-    acts, panel, rot, part, part_in, sq, sq_in, load_sem, rs, rr, ls, lr, s1, r1, s2, r2,
+    lengths_hbm, ids_hbm, acts_hbm, grads_hbm, basis_hbm, rank_basis_hbm, out,
+    lengths, ids, grads, rank_basis, acts, panel, rot, part, part_in, sq, sq_in, load_sem, rs, rr, ls, lr, s1, r1, s2, r2,
 ):
     z = lax.axis_index("blk")
     o = lax.axis_index("own")
@@ -28,10 +28,15 @@
     lanes = seqs * adapters * rank
     half = adapters * rank
 
-    load_acts = pltpu.make_async_copy(acts_hbm.at[0], acts, load_sem.at[0])
-    load_acts.start()
-    load_own = pltpu.make_async_copy(basis_hbm, panel.at[z], load_sem.at[1])
-    load_own.start()
+    loads = [
+        pltpu.make_async_copy(src, dst, load_sem.at[k])
+        for k, (src, dst) in enumerate((
+            (lengths_hbm, lengths), (ids_hbm, ids), (grads_hbm, grads),
+            (rank_basis_hbm, rank_basis), (basis_hbm, panel.at[z]), (acts_hbm.at[0], acts),
+        ))
+    ]
+    for load in loads:
+        load.start()
 
     barrier = pltpu.get_barrier_semaphore()
 
@@ -93,6 +98,9 @@
         @pl.when(z > 0)
         def _():
             left(0, c, True).start()
+
+    for load in loads[:4]:
+        load.wait()
 
     lane = lax.broadcasted_iota(jnp.int32, (1, lanes), 1)
     lane_seq = lane // half
@@ -116,8 +124,8 @@
     scale = (1.0 - forget_rate) / counts
     spread = jnp.concatenate([rank_basis[a] for a in range(adapters)] * seqs, axis=1)
     spread = jnp.where(lane_id == lane_adapter, spread, 0.0)
-    weights = jnp.dot(
-        grads[0].astype(jnp.float32), spread, precision=HIGHEST,
+    weights = lax.dot_general(
+        grads[0].astype(jnp.float32), spread, (((0,), (0,)), ((), ())), precision=HIGHEST,
         preferred_element_type=jnp.float32,
     )
     token = lax.broadcasted_iota(jnp.int32, (tokens, lanes), 0)
@@ -143,8 +151,8 @@
             for k in range(own_n):
                 part[k, block] = sums[k * share:(k + 1) * share]
 
-    load_acts.wait()
-    load_own.wait()
+    for load in loads[4:]:
+        load.wait()
     for c in range(chunks):
         add(z, c)
 
@@ -244,7 +252,8 @@
         lax.fori_loop(1, n, begin, 0)
         result = lax.fori_loop(1, n, gather, sq[z])
         lax.fori_loop(1, n, end, 0)
-    out[...] = result
+    for a in range(adapters):
+        out[a] = result[:, a * rank:(a + 1) * rank]
     for k in range(1, own_n):
         give(k).wait_send()
     over_steps(settle)
@@ -262,16 +271,19 @@
     lanes = seqs * adapters * rank
     chunks = 4 if n <= 8 else 1
     vmem = pl.BlockSpec(memory_space=pltpu.VMEM)
-    smem = pl.BlockSpec(memory_space=pltpu.SMEM)
-    anywhere = pl.BlockSpec(memory_space=pl.ANY)
+    hbm = pl.BlockSpec(memory_space=pltpu.HBM)
     dma = pltpu.SemaphoreType.DMA
     f32 = jnp.float32
     sums = pl.pallas_call(
         functools.partial(kernel, n, own_n, chunks),
-        out_shape=jax.ShapeDtypeStruct((share, lanes), f32),
-        in_specs=[smem, smem, anywhere, vmem, anywhere, vmem],
+        out_shape=jax.ShapeDtypeStruct((adapters, share, rank), f32),
+        in_specs=[hbm] * 6,
         out_specs=vmem,
         scratch_shapes=[
+            pltpu.SMEM(lengths.shape, jnp.int32),
+            pltpu.SMEM(adapter_ids.shape, jnp.int32),
+            pltpu.VMEM((1, rank, tokens), jnp.bfloat16),
+            pltpu.VMEM(rank_basis.shape, f32),
             pltpu.VMEM((tokens, width), jnp.bfloat16),
             pltpu.VMEM((n, cols, width), jnp.bfloat16),
             pltpu.VMEM((n, tokens, cols), f32),
@@ -279,18 +291,21 @@
             pltpu.VMEM((own_n - 1, n, share, lanes), f32),
             pltpu.VMEM((n, share, lanes), f32),
             pltpu.VMEM((n - 1, share, lanes), f32),
-            dma((2,)),
+            dma((6,)),
             dma((n - 1, chunks)), dma((n - 1, chunks)),
             dma((n - 1, chunks)), dma((n - 1, chunks)),
             dma((own_n - 1,)), dma((own_n - 1,)),
             dma((n - 1,)), dma((n - 1,)),
         ],
         compiler_params=pltpu.CompilerParams(
-            collective_id=0, has_side_effects=True, vmem_limit_bytes=48 << 20
+            collective_id=0, has_side_effects=True, vmem_limit_bytes=64 << 20
         ),
-    )(lengths, adapter_ids, activations, rank_grads, input_basis, rank_basis)
-    mean_sq = sums[:, :adapters * rank].T.reshape(adapters, rank, share)
-    return mean_sq + forget_rate * prior_values
+    )(
+        lengths, adapter_ids, activations, jnp.transpose(rank_grads, (0, 2, 1)), input_basis,
+        rank_basis,
+    )
+    prior = jnp.transpose(prior_values, (0, 2, 1))
+    return jnp.transpose(sums + forget_rate * prior, (0, 2, 1))
 
 
 def solution(mesh):

time: 35.5 us -> 30.5 us (0.86)
  local copies, waits for them, and re-layouts: 5.41 us -> 0 us
  other arithmetic: 0.61 us -> 1.32 us
    unnamed x13 -> x0, local copies, waits for them, and re-layouts: 5.32 us -> none
    transpose x0 -> x1, other arithmetic: none -> 1.32 us  [per_device(): return jnp.transpose(sums + forget_rate * prior, (0, 2, 1))]
    add x1 -> x0, other arithmetic: 0.61 us -> none  [per_device(): return mean_sq + forget_rate * prior_values]
where the time goes in v2:
time: 30.5 us; the launch traced here: 30.3 us
  Pallas kernels  29 us (95%)
  other arithmetic  1.32 us (4%)
    pallas_call x1, Pallas kernels, per_device(): pl.pallas_call(functools.partial(kernel, n, own_n, chunks), out_shape=jax...  29 us
    transpose x1, other arithmetic, per_device(): return jnp.transpose(sums + forget_rate * prior, (0, 2, 1))  1.32 us

profile of v2, /device:TPU:0, one launch (start us, length us, event | category | flops | bytes accessed | tf_op | source)
XLA Modules:
  0.0 30.3 jit_solution(9575866125182377454)
XLA Ops:
  0.0 29.0 %shard_map.73 = f32[4,4,16]{2,1,0:T(4,128)} custom-call(s32[1,1,2]{2,1,0:T(1,128)} %lengths_hbm.1, s32[1,8]{1,0:T(1,128)} %ids_hbm.1, bf16[1,128,7168]{2,1,0:T(8,128)(2,1)} %acts_hbm.1, bf16[1,16,128]{2,1,0:T(8,128)(2,1)} %bitcast.7, bf16[16,7168]{1,0:T(8,128)(2,1)} %basis_hbm.1, f32[4,16,16]{2,1,0:T(8,128)} %rank_basis_hbm.1), custom_call_target="tpu_custom_call" | custom-call | tf_op jit(solution)/shard_map/pallas_call | solution.py:277
  29.0 1.3 %fusion = f32[4,16,4]{1,2,0:T(4,128)} fusion(f32[4,4,16]{2,1,0:T(4,128)} %shard_map.73, f32[4,16,4]{1,2,0:T(4,128)} %param.13), kind=kLoop, calls=%fused_computation.1 | loop fusion | flops 512 | bytes 3072 | tf_op jit(solution)/shard_map/transpose | solution.py:308

commit v3 on v2

--- a/solution.py
+++ b/solution.py
@@ -14,8 +14,8 @@
 
 def kernel(
     n, own_n, chunks,
-    lengths_hbm, ids_hbm, acts_hbm, grads_hbm, basis_hbm, rank_basis_hbm, out,
-    lengths, ids, grads, rank_basis, acts, panel, rot, part, part_in, sq, sq_in, load_sem, rs, rr, ls, lr, s1, r1, s2, r2,
+    lengths_hbm, ids_hbm, acts_hbm, grads_hbm, basis_hbm, rank_basis_hbm, prior_hbm, out,
+    lengths, ids, grads, rank_basis, prior, acts, panel, rot, part, part_in, load_sem, rs, rr, ls, lr, send, recv,
 ):
     z = lax.axis_index("blk")
     o = lax.axis_index("own")
@@ -32,7 +32,7 @@
         pltpu.make_async_copy(src, dst, load_sem.at[k])
         for k, (src, dst) in enumerate((
             (lengths_hbm, lengths), (ids_hbm, ids), (grads_hbm, grads),
-            (rank_basis_hbm, rank_basis), (basis_hbm, panel.at[z]), (acts_hbm.at[0], acts),
+            (rank_basis_hbm, rank_basis), (prior_hbm, prior), (basis_hbm, panel.at[z]), (acts_hbm.at[0], acts),
         ))
     ]
     for load in loads:
@@ -40,18 +40,20 @@
 
     barrier = pltpu.get_barrier_semaphore()
 
-    def greet_blk(k, carry):
-        pl.semaphore_signal(
-            barrier, inc=1, device_id={"blk": lax.rem(z + k, n)}, device_id_type=MESH
-        )
-        return carry
-
-    lax.fori_loop(1, n, greet_blk, 0)
+    @pl.when(z < n - 1)
+    def _():
+        pl.semaphore_signal(barrier, inc=1, device_id={"blk": z + 1}, device_id_type=MESH)
+
+    @pl.when(z > 0)
+    def _():
+        pl.semaphore_signal(barrier, inc=1, device_id={"blk": z - 1}, device_id_type=MESH)
+
     for k in range(1, own_n):
         pl.semaphore_signal(
             barrier, inc=1, device_id={"own": lax.rem(o + k, own_n)}, device_id_type=MESH
         )
-    pl.semaphore_wait(barrier, n - 1 + own_n - 1)
+    neighbours = jnp.where(z > 0, 1, 0) + jnp.where(z < n - 1, 1, 0)
+    pl.semaphore_wait(barrier, neighbours + own_n - 1)
 
     def piece(c):
         return pl.ds(c * wide, wide)
@@ -99,7 +101,7 @@
         def _():
             left(0, c, True).start()
 
-    for load in loads[:4]:
+    for load in loads[:5]:
         load.wait()
 
     lane = lax.broadcasted_iota(jnp.int32, (1, lanes), 1)
@@ -131,6 +133,15 @@
     token = lax.broadcasted_iota(jnp.int32, (tokens, lanes), 0)
     weights = jnp.where((token >= lane_start) & (token < lane_end), weights, 0.0)
 
+    def give(block, k):
+        return pltpu.make_async_remote_copy(
+            src_ref=part.at[block, k], dst_ref=part_in.at[z, o], send_sem=send.at[block, k],
+            recv_sem=recv.at[z, o], device_id={"blk": block, "own": k}, device_id_type=MESH,
+        )
+
+    def give_own(k):
+        return give(z, lax.rem(o + k, own_n))
+
     def rotate(block, c):
         return lax.dot_general(
             acts[:, c * wide:(c + 1) * wide], panel[block, :, c * wide:(c + 1) * wide],
@@ -149,12 +160,15 @@
                 preferred_element_type=jnp.float32,
             )
             for k in range(own_n):
-                part[k, block] = sums[k * share:(k + 1) * share]
-
-    for load in loads[4:]:
+                part[block, k] = sums[k * share:(k + 1) * share]
+
+    for load in loads[5:]:
         load.wait()
     for c in range(chunks):
         add(z, c)
+    for k in range(1, own_n):
+        give_own(k).start()
+    part_in[z, o] = part[z, o]
 
     def step(s):
         for c in range(chunks):
@@ -177,10 +191,16 @@
             @pl.when(z - 1 - s >= 0)
             def _():
                 add(z - 1 - s, c)
+                if c == chunks - 1:
+                    for k in range(own_n):
+                        give(z - 1 - s, k).start()
 
             @pl.when(z + 1 + s < n)
             def _():
                 add(z + 1 + s, c)
+                if c == chunks - 1:
+                    for k in range(own_n):
+                        give(z + 1 + s, k).start()
 
     def settle(s):
         for c in range(chunks):
@@ -201,61 +221,48 @@
 
     over_steps(step)
 
-    def give(k):
-        to = lax.rem(o + k, own_n)
-        return pltpu.make_async_remote_copy(
-            src_ref=part.at[to], dst_ref=part_in.at[k - 1], send_sem=s1.at[k - 1],
-            recv_sem=r1.at[k - 1], device_id={"own": to}, device_id_type=MESH,
+    def source(zs, k):
+        return pltpu.make_async_remote_copy(
+            src_ref=part_in.at[zs, k], dst_ref=part_in.at[zs, k], send_sem=send.at[zs, k],
+            recv_sem=recv.at[zs, k], device_id={"blk": zs, "own": k}, device_id_type=MESH,
         )
 
     for k in range(1, own_n):
-        give(k).start()
-    total = part[o]
-    for k in range(1, own_n):
-        give(k).wait_recv()
-        total = total + part_in[k - 1]
-    squares = total * total * scale
-    folded = squares
-    for q in range(1, seqs):
-        folded = folded + pltpu.roll(squares, q * half, 2)
-    sq[...] = folded
-
-    def give_sq(k):
-        to = lax.rem(z + k, n)
-        return pltpu.make_async_remote_copy(
-            src_ref=sq.at[to], dst_ref=sq_in.at[k - 1], send_sem=s2.at[k - 1],
-            recv_sem=r2.at[k - 1], device_id={"blk": to}, device_id_type=MESH,
-        )
-
+        source(z, lax.rem(o + k, own_n)).wait_recv()
+
+    def squares(zs):
+        total = part_in[zs, 0]
+        for k in range(1, own_n):
+            total = total + part_in[zs, k]
+        return total * total
+
+    def gather(k, value):
+        zs = lax.rem(z + k, n)
+        for q in range(own_n):
+            source(zs, q).wait_recv()
+        return value + squares(zs)
+
+    def settle_sums(k, carry):
+        for q in range(own_n):
+            give(lax.rem(z + k, n), q).wait_send()
+        return carry
+
+    result = squares(z)
     if n <= 8:
         for k in range(1, n):
-            give_sq(k).start()
-        result = sq[z]
-        for k in range(1, n):
-            give_sq(k).wait_recv()
-            result = result + sq_in[k - 1]
-        for k in range(1, n):
-            give_sq(k).wait_send()
+            result = gather(k, result)
     else:
-        def begin(k, carry):
-            give_sq(k).start()
-            return carry
-
-        def gather(k, value):
-            give_sq(k).wait_recv()
-            return value + sq_in[k - 1]
-
-        def end(k, carry):
-            give_sq(k).wait_send()
-            return carry
-
-        lax.fori_loop(1, n, begin, 0)
-        result = lax.fori_loop(1, n, gather, sq[z])
-        lax.fori_loop(1, n, end, 0)
+        result = lax.fori_loop(1, n, gather, result)
+    result = result * scale
+    folded = result
+    for q in range(1, seqs):
+        folded = folded + pltpu.roll(result, q * half, 1)
+    result = folded
     for a in range(adapters):
-        out[a] = result[:, a * rank:(a + 1) * rank]
+        out[a] = result[:, a * rank:(a + 1) * rank] + forget_rate * prior[a]
     for k in range(1, own_n):
-        give(k).wait_send()
+        give_own(k).wait_send()
+    lax.fori_loop(1, n, settle_sums, 0)
     over_steps(settle)
 
 
@@ -277,35 +284,32 @@
     sums = pl.pallas_call(
         functools.partial(kernel, n, own_n, chunks),
         out_shape=jax.ShapeDtypeStruct((adapters, share, rank), f32),
-        in_specs=[hbm] * 6,
+        in_specs=[hbm] * 7,
         out_specs=vmem,
         scratch_shapes=[
             pltpu.SMEM(lengths.shape, jnp.int32),
             pltpu.SMEM(adapter_ids.shape, jnp.int32),
             pltpu.VMEM((1, rank, tokens), jnp.bfloat16),
             pltpu.VMEM(rank_basis.shape, f32),
+            pltpu.VMEM((adapters, share, rank), f32),
             pltpu.VMEM((tokens, width), jnp.bfloat16),
             pltpu.VMEM((n, cols, width), jnp.bfloat16),
             pltpu.VMEM((n, tokens, cols), f32),
-            pltpu.VMEM((own_n, n, share, lanes), f32),
-            pltpu.VMEM((own_n - 1, n, share, lanes), f32),
-            pltpu.VMEM((n, share, lanes), f32),
-            pltpu.VMEM((n - 1, share, lanes), f32),
-            dma((6,)),
+            pltpu.VMEM((n, own_n, share, lanes), f32),
+            pltpu.VMEM((n, own_n, share, lanes), f32),
+            dma((7,)),
             dma((n - 1, chunks)), dma((n - 1, chunks)),
             dma((n - 1, chunks)), dma((n - 1, chunks)),
-            dma((own_n - 1,)), dma((own_n - 1,)),
-            dma((n - 1,)), dma((n - 1,)),
+            dma((n, own_n)), dma((n, own_n)),
         ],
         compiler_params=pltpu.CompilerParams(
             collective_id=0, has_side_effects=True, vmem_limit_bytes=64 << 20
         ),
     )(
         lengths, adapter_ids, activations, jnp.transpose(rank_grads, (0, 2, 1)), input_basis,
-        rank_basis,
+        rank_basis, jnp.transpose(prior_values, (0, 2, 1)),
     )
-    prior = jnp.transpose(prior_values, (0, 2, 1))
-    return jnp.transpose(sums + forget_rate * prior, (0, 2, 1))
+    return jnp.transpose(sums, (0, 2, 1))
 
 
 def solution(mesh):

time: 30.5 us -> 28.9 us (0.948)
  Pallas kernels: 29 us -> 27.4 us
  other arithmetic: 1.32 us -> 0 us
  local copies, waits for them, and re-layouts: 0 us -> 1.3 us
    pallas_call x1, Pallas kernels: 29 us -> 27.4 us  [per_device(): pl.pallas_call(functools.partial(kernel, n, own_n, chunks), out_shape=jax...]
    transpose x1 -> x0, other arithmetic: 1.32 us -> none  [per_device(): return jnp.transpose(sums + forget_rate * prior, (0, 2, 1))]
    unnamed x0 -> x1, local copies, waits for them, and re-layouts: none -> 1.3 us
where the time goes in v3:
time: 28.9 us; the launch traced here: 28.7 us
  Pallas kernels  27.4 us (95%)
  local copies, waits for them, and re-layouts  1.3 us (4%)
    pallas_call x1, Pallas kernels, per_device(): pl.pallas_call(functools.partial(kernel, n, own_n, chunks), out_shape=jax...  27.4 us
    unnamed x1, local copies, waits for them, and re-layouts  1.3 us

profile of v3, /device:TPU:0, one launch (start us, length us, event | category | flops | bytes accessed | tf_op | source)
XLA Modules:
  0.0 28.7 jit_solution(15095106924022237639)
XLA Ops:
  0.0 27.4 %shard_map.73 = f32[4,4,16]{2,1,0:T(4,128)} custom-call(s32[1,1,2]{2,1,0:T(1,128)} %lengths_hbm.1, s32[1,8]{1,0:T(1,128)} %ids_hbm.1, bf16[1,128,7168]{2,1,0:T(8,128)(2,1)} %acts_hbm.1, bf16[1,16,128]{2,1,0:T(8,128)(2,1)} %bitcast.5, bf16[16,7168]{1,0:T(8,128)(2,1)} %basis_hbm.1, f32[4,16,16]{2,1,0:T(8,128)} %rank_basis_hbm.1, f32[4,4,16]{2,1,0:T(4,128)} %bitcast.4), custom_call_target="tpu_custom_call" | custom-call | tf_op jit(solution)/shard_map/pallas_call | solution.py:284
  27.4 1.3 %copy.9 = f32[4,16,4]{1,2,0:T(4,128)} copy(f32[4,16,4]{1,2,0:T(4,128)} %bitcast.3) | data formatting | bytes 2048

commit v4 on v3

--- a/solution.py
+++ b/solution.py
@@ -13,16 +13,18 @@
 
 
 def kernel(
-    n, own_n, chunks,
+    n, own_n, pieces, helped,
     lengths_hbm, ids_hbm, acts_hbm, grads_hbm, basis_hbm, rank_basis_hbm, prior_hbm, out,
     lengths, ids, grads, rank_basis, prior, acts, panel, rot, part, part_in, load_sem, rs, rr, ls, lr, send, recv,
+    up, up_in, aid, aid_in, up_sem, aid_send, aid_recv,
 ):
     z = lax.axis_index("blk")
     o = lax.axis_index("own")
     tokens, width = acts.shape
     cols = panel.shape[1]
     share = cols // own_n
-    wide = width // chunks
+    chunks = len(pieces)
+    bf16, f32 = jnp.bfloat16, jnp.float32
     seqs = lengths.shape[2]
     adapters, rank = rank_basis.shape[0], rank_basis.shape[1]
     lanes = seqs * adapters * rank
@@ -56,7 +58,21 @@
     pl.semaphore_wait(barrier, neighbours + own_n - 1)
 
     def piece(c):
-        return pl.ds(c * wide, wide)
+        return pl.ds(*pieces[c])
+
+    def goes_right(c):
+        return z < (n - 2 if helped and c == 0 else n - 1)
+
+    def goes_left(c):
+        return z > (1 if helped and c == 0 else 0)
+
+    def comes_left(s, c):
+        there = z - 1 - s >= 0
+        return there & (z < n - 1) if helped and c == 0 else there
+
+    def comes_right(s, c):
+        there = z + 1 + s < n
+        return there & (z > 0) if helped and c == 0 else there
 
     def right(s, c, first=False):
         at = (slice(None), piece(c))
@@ -93,11 +109,11 @@
         )
 
     for c in range(chunks):
-        @pl.when(z < n - 1)
+        @pl.when(goes_right(c))
         def _():
             right(0, c, True).start()
 
-        @pl.when(z > 0)
+        @pl.when(goes_left(c))
         def _():
             left(0, c, True).start()
 
@@ -144,14 +160,12 @@
 
     def rotate(block, c):
         return lax.dot_general(
-            acts[:, c * wide:(c + 1) * wide], panel[block, :, c * wide:(c + 1) * wide],
+            acts[:, piece(c)], panel[block, :, piece(c)],
             (((1,), (1,)), ((), ())), preferred_element_type=jnp.float32,
         )
 
     def add(block, c):
-        value = rotate(block, c)
-        if c > 0:
-            value = value + rot[block]
+        value = rotate(block, c) + rot[block]
         if c < chunks - 1:
             rot[block] = value
         else:
@@ -164,6 +178,102 @@
 
     for load in loads[5:]:
         load.wait()
+    rot[...] = jnp.zeros_like(rot)
+    end = jnp.where(z < n // 2, 0, n - 1)
+    side = jnp.where(z < n // 2, 0, 1)
+    is_end = (z == 0) | (z == n - 1)
+    is_aid = (z == 1) | (z == n - 2)
+    other = jnp.where(z < n // 2, 1 - z, 2 * n - 3 - z)
+
+    def send_up():
+        return pltpu.make_async_remote_copy(
+            src_ref=up, dst_ref=up_in, send_sem=up_sem.at[0], recv_sem=up_sem.at[1],
+            device_id={"blk": other}, device_id_type=MESH,
+        )
+
+    if helped:
+        @pl.when(is_end)
+        def _():
+            rows = jnp.concatenate(
+                [
+                    sum(
+                        weights[:, (q * adapters + a) * rank:(q * adapters + a + 1) * rank]
+                        for a in range(adapters)
+                    )
+                    for q in range(seqs)
+                ],
+                axis=1,
+            )
+            terms, rest = [], rows
+            for _ in range(3):
+                term = rest.astype(bf16)
+                terms.append(lax.dot_general(
+                    term, acts[:, piece(0)], (((0,), (0,)), ((), ())),
+                    preferred_element_type=f32,
+                ))
+                rest = rest - term.astype(f32)
+            grouped = terms[2] + terms[1] + terms[0]
+            high = grouped.astype(bf16)
+            up[:seqs * rank] = high
+            up[seqs * rank:] = (grouped - high.astype(f32)).astype(bf16)
+            send_up().start()
+
+    def give_aid(block, k):
+        return pltpu.make_async_remote_copy(
+            src_ref=aid.at[block, k], dst_ref=aid_in.at[side, o], send_sem=aid_send.at[block, k],
+            recv_sem=aid_recv.at[side, o], device_id={"blk": block, "own": k},
+            device_id_type=MESH,
+        )
+
+    def aid_block(k):
+        return jnp.where(end == 0, n - k, k - 1)
+
+    def help_end():
+        send_up().wait_recv()
+        for k in range(1, n):
+            block = aid_block(k)
+            both = lax.dot_general(
+                panel[block, :, piece(0)], up_in[...], (((1,), (1,)), ((), ())),
+                preferred_element_type=f32,
+            )
+            sums = both[:, :seqs * rank] + both[:, seqs * rank:]
+            sums = jnp.concatenate(
+                [
+                    sums[:, q * rank:(q + 1) * rank]
+                    for q in range(seqs) for _ in range(adapters)
+                ],
+                axis=1,
+            )
+            end_id = jnp.zeros((1, lanes), jnp.int32)
+            for q in range(seqs):
+                end_id = jnp.where(lane_seq == q, ids[0, end * seqs + q], end_id)
+            sums = jnp.where(end_id == lane_adapter, sums, 0.0)
+            for j in range(own_n):
+                aid[block, j] = sums[j * share:(j + 1) * share]
+            for j in range(own_n):
+                @pl.when((block != z) | (o != j))
+                def _():
+                    give_aid(block, j).start()
+
+            @pl.when(block == z)
+            def _():
+                aid_in[side, o] = aid[z, o]
+
+    def settle_aid():
+        for k in range(1, n):
+            block = aid_block(k)
+            for j in range(own_n):
+                @pl.when((block != z) | (o != j))
+                def _():
+                    give_aid(block, j).wait_send()
+
+    def from_aid(which, k):
+        return pltpu.make_async_remote_copy(
+            src_ref=aid_in.at[which, k], dst_ref=aid_in.at[which, k],
+            send_sem=aid_recv.at[which, k], recv_sem=aid_recv.at[which, k],
+            device_id={"blk": other, "own": k}, device_id_type=MESH,
+        )
+
     for c in range(chunks):
         add(z, c)
     for k in range(1, own_n):
@@ -172,30 +282,30 @@
 
     def step(s):
         for c in range(chunks):
-            @pl.when(z - 1 - s >= 0)
+            @pl.when(comes_left(s, c))
             def _():
                 from_left(s, c).wait_recv()
 
-                @pl.when(z < n - 1)
+                @pl.when(goes_right(c))
                 def _():
                     right(s + 1, c).start()
 
-            @pl.when(z + 1 + s < n)
+            @pl.when(comes_right(s, c))
             def _():
                 from_right(s, c).wait_recv()
 
-                @pl.when(z > 0)
+                @pl.when(goes_left(c))
                 def _():
                     left(s + 1, c).start()
 
-            @pl.when(z - 1 - s >= 0)
+            @pl.when(comes_left(s, c))
             def _():
                 add(z - 1 - s, c)
                 if c == chunks - 1:
                     for k in range(own_n):
                         give(z - 1 - s, k).start()
 
-            @pl.when(z + 1 + s < n)
+            @pl.when(comes_right(s, c))
             def _():
                 add(z + 1 + s, c)
                 if c == chunks - 1:
@@ -204,11 +314,11 @@
 
     def settle(s):
         for c in range(chunks):
-            @pl.when((z - s >= 0) & (z < n - 1))
+            @pl.when((z - s >= 0) & goes_right(c))
             def _():
                 right(s, c).wait_send()
 
-            @pl.when((z + s < n) & (z > 0))
+            @pl.when((z + s < n) & goes_left(c))
             def _():
                 left(s, c).wait_send()
 
@@ -220,6 +330,8 @@
             lax.fori_loop(0, n - 1, lambda s, carry: (f(s), carry)[1], 0)
 
     over_steps(step)
+    if helped:
+        pl.when(is_aid)(help_end)
 
     def source(zs, k):
         return pltpu.make_async_remote_copy(
@@ -234,6 +346,12 @@
         total = part_in[zs, 0]
         for k in range(1, own_n):
             total = total + part_in[zs, k]
+        if helped:
+            more = aid_in[jnp.where(zs == 0, 0, 1), 0]
+            for k in range(1, own_n):
+                more = more + aid_in[jnp.where(zs == 0, 0, 1), k]
+            helps = jnp.where(((zs == 0) | (zs == n - 1)) & (zs != z), 1, 0)
+            total = total + jnp.where(jnp.full(total.shape, helps) == 1, more, 0.0)
         return total * total
 
     def gather(k, value):
@@ -247,12 +365,23 @@
             give(lax.rem(z + k, n), q).wait_send()
         return carry
 
-    result = squares(z)
     if n <= 8:
         for k in range(1, n):
-            result = gather(k, result)
+            for q in range(own_n):
+                source(lax.rem(z + k, n), q).wait_recv()
+        if helped:
+            for which in range(2):
+                for q in range(own_n):
+                    mine = (z == (1, n - 2)[which]) & (o == q)
+
+                    @pl.when((z != (0, n - 1)[which]) & jnp.logical_not(mine))
+                    def _():
+                        from_aid(which, q).wait_recv()
+        result = squares(z)
+        for k in range(1, n):
+            result = result + squares(lax.rem(z + k, n))
     else:
-        result = lax.fori_loop(1, n, gather, result)
+        result = lax.fori_loop(1, n, gather, squares(z))
     result = result * scale
     folded = result
     for q in range(1, seqs):
@@ -263,7 +392,25 @@
     for k in range(1, own_n):
         give_own(k).wait_send()
     lax.fori_loop(1, n, settle_sums, 0)
+    if helped:
+        @pl.when(is_end)
+        def _():
+            send_up().wait_send()
+
+        pl.when(is_aid)(settle_aid)
     over_steps(settle)
+
+
+def cut(width, n, helped):
+    if n > 8:
+        return ((0, width),)
+    tiles = width // 128
+    first = max(1, tiles * 2 // 7) if helped else 0
+    count = 4
+    edges = [first + (tiles - first) * k // count for k in range(count + 1)]
+    if helped:
+        edges = [0] + edges
+    return tuple((int(a * 128), int((b - a) * 128)) for a, b in zip(edges, edges[1:]))
 
 
 def per_device(
@@ -276,13 +423,17 @@
     seqs = lengths.shape[2]
     adapters, rank = rank_basis.shape[:2]
     lanes = seqs * adapters * rank
-    chunks = 4 if n <= 8 else 1
+    helped = 4 <= n <= 8
+    pieces = cut(width, n, helped)
+    chunks = len(pieces)
+    first = pieces[0][1] if helped else 128
+    terms = 2 * seqs * rank
     vmem = pl.BlockSpec(memory_space=pltpu.VMEM)
     hbm = pl.BlockSpec(memory_space=pltpu.HBM)
     dma = pltpu.SemaphoreType.DMA
     f32 = jnp.float32
     sums = pl.pallas_call(
-        functools.partial(kernel, n, own_n, chunks),
+        functools.partial(kernel, n, own_n, pieces, helped),
         out_shape=jax.ShapeDtypeStruct((adapters, share, rank), f32),
         in_specs=[hbm] * 7,
         out_specs=vmem,
@@ -301,6 +452,11 @@
             dma((n - 1, chunks)), dma((n - 1, chunks)),
             dma((n - 1, chunks)), dma((n - 1, chunks)),
             dma((n, own_n)), dma((n, own_n)),
+            pltpu.VMEM((terms, first), jnp.bfloat16),
+            pltpu.VMEM((terms, first), jnp.bfloat16),
+            pltpu.VMEM((n if helped else 1, own_n, share, lanes), f32),
+            pltpu.VMEM((2, own_n, share, lanes), f32),
+            dma((2,)), dma((n, own_n)), dma((2, own_n)),
         ],
         compiler_params=pltpu.CompilerParams(
             collective_id=0, has_side_effects=True, vmem_limit_bytes=64 << 20

time: 28.9 us -> 26.7 us (0.924)
  Pallas kernels: 27.4 us -> 25.2 us
    pallas_call x1, Pallas kernels: 27.4 us -> 25.2 us  [per_device(): pl.pallas_call(functools.partial(kernel, n, own_n, pieces, helped), out_s...]
where the time goes in v4:
time: 26.7 us; the launch traced here: 26.5 us
  Pallas kernels  25.2 us (94%)
  local copies, waits for them, and re-layouts  1.3 us (5%)
    pallas_call x1, Pallas kernels, per_device(): pl.pallas_call(functools.partial(kernel, n, own_n, pieces, helped), out_s...  25.2 us
    unnamed x1, local copies, waits for them, and re-layouts  1.3 us

profile of v4, /device:TPU:0, one launch (start us, length us, event | category | flops | bytes accessed | tf_op | source)
XLA Modules:
  0.0 26.5 jit_solution(1026378633268849611)
XLA Ops:
  0.0 25.2 %shard_map.73 = f32[4,4,16]{2,1,0:T(4,128)} custom-call(s32[1,1,2]{2,1,0:T(1,128)} %lengths_hbm.1, s32[1,8]{1,0:T(1,128)} %ids_hbm.1, bf16[1,128,7168]{2,1,0:T(8,128)(2,1)} %acts_hbm.1, bf16[1,16,128]{2,1,0:T(8,128)(2,1)} %bitcast.5, bf16[16,7168]{1,0:T(8,128)(2,1)} %basis_hbm.1, f32[4,16,16]{2,1,0:T(8,128)} %rank_basis_hbm.1, f32[4,4,16]{2,1,0:T(4,128)} %bitcast.4), custom_call_target="tpu_custom_call" | custom-call | tf_op jit(solution)/shard_map/pallas_call | solution.py:435
  25.2 1.3 %copy.9 = f32[4,16,4]{1,2,0:T(4,128)} copy(f32[4,16,4]{1,2,0:T(4,128)} %bitcast.3) | data formatting | bytes 2048

commit v5 on v4

--- a/solution.py
+++ b/solution.py
@@ -37,8 +37,6 @@
             (rank_basis_hbm, rank_basis), (prior_hbm, prior), (basis_hbm, panel.at[z]), (acts_hbm.at[0], acts),
         ))
     ]
-    for load in loads:
-        load.start()
 
     barrier = pltpu.get_barrier_semaphore()
 
@@ -54,6 +52,8 @@
         pl.semaphore_signal(
             barrier, inc=1, device_id={"own": lax.rem(o + k, own_n)}, device_id_type=MESH
         )
+    for load in loads:
+        load.start()
     neighbours = jnp.where(z > 0, 1, 0) + jnp.where(z < n - 1, 1, 0)
     pl.semaphore_wait(barrier, neighbours + own_n - 1)
 
@@ -160,7 +160,7 @@
 
     def rotate(block, c):
         return lax.dot_general(
-            acts[:, piece(c)], panel[block, :, piece(c)],
+            panel[block, :, piece(c)], acts[:, piece(c)],
             (((1,), (1,)), ((), ())), preferred_element_type=jnp.float32,
         )
 
@@ -170,7 +170,7 @@
             rot[block] = value
         else:
             sums = lax.dot_general(
-                value, weights, (((0,), (0,)), ((), ())), precision=HIGHEST,
+                value, weights, (((1,), (0,)), ((), ())), precision=HIGHEST,
                 preferred_element_type=jnp.float32,
             )
             for k in range(own_n):
@@ -230,34 +230,35 @@
 
     def help_end():
         send_up().wait_recv()
+        rows = n * cols
+        both = lax.dot_general(
+            panel[:, :, piece(0)].reshape(rows, pieces[0][1]), up_in[...],
+            (((1,), (1,)), ((), ())), preferred_element_type=f32,
+        )
+        sums = both[:, :seqs * rank] + both[:, seqs * rank:]
+        sums = jnp.concatenate(
+            [
+                sums[:, q * rank:(q + 1) * rank]
+                for q in range(seqs) for _ in range(adapters)
+            ],
+            axis=1,
+        )
+        end_id = jnp.zeros((1, lanes), jnp.int32)
+        for q in range(seqs):
+            end_id = jnp.where(lane_seq == q, ids[0, end * seqs + q], end_id)
+        sums = jnp.where(end_id == lane_adapter, sums, 0.0)
+        for k in range(n):
+            for j in range(own_n):
+                at = k * cols + j * share
+                aid[k, j] = sums[at:at + share]
         for k in range(1, n):
             block = aid_block(k)
-            both = lax.dot_general(
-                panel[block, :, piece(0)], up_in[...], (((1,), (1,)), ((), ())),
-                preferred_element_type=f32,
-            )
-            sums = both[:, :seqs * rank] + both[:, seqs * rank:]
-            sums = jnp.concatenate(
-                [
-                    sums[:, q * rank:(q + 1) * rank]
-                    for q in range(seqs) for _ in range(adapters)
-                ],
-                axis=1,
-            )
-            end_id = jnp.zeros((1, lanes), jnp.int32)
-            for q in range(seqs):
-                end_id = jnp.where(lane_seq == q, ids[0, end * seqs + q], end_id)
-            sums = jnp.where(end_id == lane_adapter, sums, 0.0)
-            for j in range(own_n):
-                aid[block, j] = sums[j * share:(j + 1) * share]
             for j in range(own_n):
                 @pl.when((block != z) | (o != j))
                 def _():
                     give_aid(block, j).start()
 
-            @pl.when(block == z)
-            def _():
-                aid_in[side, o] = aid[z, o]
+        aid_in[side, o] = aid[z, o]
 
     def settle_aid():
         for k in range(1, n):
@@ -445,7 +446,7 @@
             pltpu.VMEM((adapters, share, rank), f32),
             pltpu.VMEM((tokens, width), jnp.bfloat16),
             pltpu.VMEM((n, cols, width), jnp.bfloat16),
-            pltpu.VMEM((n, tokens, cols), f32),
+            pltpu.VMEM((n, cols, tokens), f32),
             pltpu.VMEM((n, own_n, share, lanes), f32),
             pltpu.VMEM((n, own_n, share, lanes), f32),
             dma((7,)),

time: 26.7 us -> 26.6 us (level)
  no operation moved by 1% of the time
where the time goes in v5:
time: 26.6 us; the launch traced here: 26.5 us
  Pallas kernels  25.1 us (94%)
  local copies, waits for them, and re-layouts  1.3 us (5%)
    pallas_call x1, Pallas kernels, per_device(): pl.pallas_call(functools.partial(kernel, n, own_n, pieces, helped), out_s...  25.1 us
    unnamed x1, local copies, waits for them, and re-layouts  1.3 us

profile of v5, /device:TPU:0, one launch (start us, length us, event | category | flops | bytes accessed | tf_op | source)
XLA Modules:
  0.0 26.5 jit_solution(15841543777558134080)
XLA Ops:
  0.0 25.1 %shard_map.73 = f32[4,4,16]{2,1,0:T(4,128)} custom-call(s32[1,1,2]{2,1,0:T(1,128)} %lengths_hbm.1, s32[1,8]{1,0:T(1,128)} %ids_hbm.1, bf16[1,128,7168]{2,1,0:T(8,128)(2,1)} %acts_hbm.1, bf16[1,16,128]{2,1,0:T(8,128)(2,1)} %bitcast.5, bf16[16,7168]{1,0:T(8,128)(2,1)} %basis_hbm.1, f32[4,16,16]{2,1,0:T(8,128)} %rank_basis_hbm.1, f32[4,4,16]{2,1,0:T(4,128)} %bitcast.4), custom_call_target="tpu_custom_call" | custom-call | tf_op jit(solution)/shard_map/pallas_call | solution.py:436
  25.2 1.3 %copy.9 = f32[4,16,4]{1,2,0:T(4,128)} copy(f32[4,16,4]{1,2,0:T(4,128)} %bitcast.3) | data formatting | bytes 2048
